TPU v7x, 256 devices: a whole 4x4x8 slice. The times are simulated.
256 devices in a mesh: dom: 16 (over y, x), feat: 16 (over z, core).
Axes of the slice: x: 4, y: 4, z: 8, core: 2. Of those that a mesh axis runs over, the one named last changes fastest.
Arguments:
- feature_table: float32 [1024, 131072], P('feat', 'dom'), may hold values from -6 to 6
- seed_ids: int32 [16384], P('dom'), may hold values from 0 to 8191
- neighbours: int32 [15, 16384], P(None, 'dom'), may hold values from 0 to 8191
- owners: int32 [1024, 1], P('dom'), may hold values from 0 to 15; in each aligned block of 64 rows (0 to 63, 64 to 127, ...) at most 8 rows name the same one
- blocks: int32 [1024], P('dom'), may hold values from 0 to 63
- counts: int32 [1024], P('dom'), may hold values from 1 to 128
- w_self: float32 [1024, 1024], P('feat'), may hold values from -0.1875 to 0.1875
- w_neigh: float32 [1024, 1024], P('feat'), may hold values from -0.5 to 0.5
- out_bias: float32 [1024], replicated, may hold values from -3 to 3
- cotangent: bfloat16 [16384, 1024], P(('dom', 'feat')), may hold values from -0.046875 to 0.046875
Outputs:
- hidden: bfloat16 [16384, 1024], P(('dom', 'feat'))
- grad_self: float32 [1024, 1024], P('feat')
- grad_neigh: float32 [1024, 1024], P('feat')
Inputs may be any that keep to these rules, and one draw needn't show every extreme that they name: `owners`: among the 64 frontier entries of one partition no owner appears more than 8 times.
All inputs are finite; a program needn't handle non-finite values.
Results may differ from a plain program's by a relative error of at most 0.003.
Values may be sent and summed in bfloat16 or wider, within the bound.
No kernel may reach another device: no remote copies, remote signals or barrier semaphores. Data moves between devices by JAX's collectives and lax.ppermute only.
A program may use at most 128 MiB of HBM per device.

v0:
```python
import jax
import jax.numpy as jnp
from jax import lax
from jax.sharding import PartitionSpec as P

FAN = 15
BLOCK = 128
SLOTS = 8


def silu_slope(preact):
    sigma = jax.nn.sigmoid(preact)
    return sigma * (1.0 + preact * (1.0 - sigma))


def contract(left, right):
    return lax.dot_general(
        left,
        right,
        (((0,), (0,)), ((), ())),
        precision=lax.Precision.HIGHEST,
        preferred_element_type=jnp.float32,
    )


def product(left, right):
    return lax.dot_general(
        left,
        right,
        (((1,), (0,)), ((), ())),
        precision=lax.Precision.HIGHEST,
        preferred_element_type=jnp.float32,
    )


def body(
    feature_table,
    seed_ids,
    neighbours,
    owners,
    blocks,
    counts,
    w_self,
    w_neigh,
    out_bias,
    cotangent,
):
    cols_dev = feature_table.shape[0]
    node_rows = feature_table.shape[1]
    n_dom = lax.axis_size("dom")
    front = owners.shape[0]
    seeds_dev = seed_ids.shape[0]
    fanout = neighbours.shape[0]
    owner_ids = owners[:, 0]
    one_hot = (owner_ids[:, None] == jnp.arange(n_dom, dtype=jnp.int32)[None, :]).astype(jnp.int32)
    slot_rank = jnp.sum(jnp.cumsum(one_hot, axis=0) * one_hot, axis=1) - 1
    outgoing_ids = jnp.zeros((n_dom, SLOTS), jnp.int32).at[owner_ids, slot_rank].set(blocks)
    requested = lax.all_to_all(outgoing_ids, "dom", split_axis=0, concat_axis=0, tiled=True)
    table_rows = jnp.transpose(feature_table)
    block_rows = table_rows.reshape(node_rows // BLOCK, BLOCK, cols_dev)
    outgoing = block_rows[requested.reshape(-1)].reshape(n_dom, SLOTS, BLOCK, cols_dev)
    arrived = lax.all_to_all(outgoing, "dom", split_axis=0, concat_axis=0, tiled=True)
    arrived_flat = arrived.reshape(n_dom * SLOTS, BLOCK, cols_dev)
    frontier = arrived_flat[owner_ids * SLOTS + slot_rank]
    row_valid = jnp.arange(BLOCK, dtype=jnp.int32)[None, :] < counts[:, None]
    frontier = jnp.where(row_valid[:, :, None], frontier, 0.0).reshape(front * BLOCK, cols_dev)
    picked = frontier[neighbours.reshape(-1)].reshape(fanout, seeds_dev, cols_dev)
    neighbour_mean = jnp.sum(picked, axis=0) * (1.0 / FAN)
    self_rows = table_rows[seed_ids]
    stacked = jnp.concatenate([self_rows, neighbour_mean], axis=1)
    weight_cat = jnp.concatenate([w_self, w_neigh], axis=0)
    preact = (
        lax.psum_scatter(product(stacked, weight_cat), "feat", scatter_dimension=0, tiled=True)
        + out_bias[None, :]
    )
    hidden = jax.nn.silu(preact).astype(jnp.bfloat16)
    slope = (cotangent.astype(jnp.float32) * silu_slope(preact)).astype(jnp.bfloat16)
    grad_local = contract(
        stacked, lax.all_gather(slope, "feat", axis=0, tiled=True).astype(jnp.float32)
    )
    grad_total = lax.psum(grad_local, "dom")
    return (hidden, grad_total[:cols_dev], grad_total[cols_dev:])


def solution(mesh):
    return jax.shard_map(
        body,
        mesh=mesh,
        in_specs=(
            P("feat", "dom"),
            P("dom"),
            P(None, "dom"),
            P("dom", None),
            P("dom"),
            P("dom"),
            P("feat", None),
            P("feat", None),
            P(),
            P(("dom", "feat"), None),
        ),
        out_specs=(P(("dom", "feat"), None), P("feat", None), P("feat", None)),
        check_vma=False,
    )
```

profile of v0, /device:TPU:32, one launch (start us, length us, event | category | flops | bytes accessed | tf_op | source)
XLA Modules:
  0.0 396.3 jit_solution(11303320467679522365)
XLA Ops:
  7.2 0.7 fusion.5
  7.9 0.1 reduce_window_sum.11
  8.0 0.8 select_reduce_fusion
  8.8 0.7 fusion.10
  9.5 5.7 %scatter_fusion = s32[16,8]{0,1:T(8,128)S(1)} fusion(s32[16,8]{0,1:T(8,128)S(1)} %broadcast_in_dim.18, s32[64]{0:T(128)S(1)} %get-tuple-element.8, s32[64]{0:T(128)} %param.14), kind=kCustom, calls=%fused_computation.4 | custom fusion | bytes 1280 | tf_op jit(solution)/shard_map/scatter | solution.py:57
  15.3 0.7 copy.24
  15.9 7.0 %all-to-all-start = ((s32[16,1,8]{2,1,0:T(1,128)}), s32[16,1,8]{2,1,0:T(1,128)S(1)}, u32[]{:S(2)}, u32[]{:S(2)}) async-start(s32[16,1,8]{2,1,0:T(1,128)} %copy.24), calls=%async_computation | async-start | bytes 16384 | tf_op jit(solution)/shard_map/all_to_all | solution.py:58
  23.0 0.7 fusion.6
  23.7 3.8 copy.23
  27.5 2.9 all-to-all-done
  30.4 0.5 broadcast.144
  31.0 0.7 reduce.3
  31.6 0.1 reshape.132
  31.7 6.5 %gather_fusion.1 = f32[128,128,64]{2,1,0:T(8,128)} fusion(f32[64,128,64]{2,1,0:T(8,128)} %bitcast.37, s32[1024]{0:T(1024)S(1)} %pad_clamp_fusion.1), kind=kCustom, calls=%fused_computation.1 | custom fusion | bytes 8389120 | tf_op jit(solution)/shard_map/gather | solution.py:61
  38.2 6.8 %copy.25 = f32[128,128,64]{1,2,0:T(8,128)} copy(f32[128,128,64]{2,1,0:T(8,128)} %gather_fusion.1) | data formatting | bytes 8388608 | tf_op jit(solution)/shard_map/gather | solution.py:61
  45.0 0.0 copy-start.5
  45.0 0.0 copy-start.3
  45.1 4.7 %all-to-all-start.1 = ((f32[16,8,128,64]{2,3,1,0:T(8,128)}), f32[16,8,128,64]{2,3,1,0:T(8,128)}, u32[]{:S(2)}, u32[]{:S(2)}) async-start(f32[16,8,128,64]{2,3,1,0:T(8,128)} %bitcast.40), calls=%async_computation.1 | async-start | bytes 8388608 | tf_op jit(solution)/shard_map/all_to_all | solution.py:62
  49.7 0.0 reduce-scatter.2.cloned.1.call-start
  49.8 0.0 copy-done.5
  49.8 0.0 copy-done.3
  49.8 0.1 copy.30
  49.9 5.0 %gather_fusion = f32[1024,64]{1,0:T(8,128)S(1)} fusion(f32[8192,64]{1,0:T(8,128)} %bitcast.38, s32[1024]{0:T(1024)S(1)} %fusion.7), kind=kCustom, calls=%fused_computation | custom fusion | bytes 528384 | tf_op jit(solution)/shard_map/gather | solution.py:69
  54.9 0.1 compare_select_fusion
  55.0 55.8 %all-to-all-done.1 = f32[16,8,128,64]{2,3,1,0:T(8,128)} async-done(((f32[16,8,128,64]{2,3,1,0:T(8,128)}), f32[16,8,128,64]{2,3,1,0:T(8,128)}, u32[]{:S(2)}, u32[]{:S(2)}) %all-to-all-start.1) | async-done | bytes 4194336 | tf_op jit(solution)/shard_map/all_to_all | solution.py:62
  110.8 2.9 gather_fusion.2
  113.7 2.7 copy.28
  116.4 7.4 %bitcast_select_fusion = f32[8192,64]{1,0:T(8,128)} fusion(f32[64,128,64]{2,1,0:T(8,128)} %copy.28, pred[8192]{0:T(1024)(128)(4,1)S(1)} %fusion.6), kind=kLoop, calls=%fused_computation.5 | loop fusion | flops 524288 | bytes 4202496 | tf_op jit(solution)/shard_map/jit(_where)/select_n | solution.py:66
  123.8 53.7 %gather_fusion.3 = f32[15360,64]{1,0:T(8,128)} fusion(f32[8192,64]{1,0:T(8,128)} %bitcast_select_fusion, s32[15360]{0:T(1024)S(1)} %broadcast_clamp_fusion), kind=kCustom, calls=%fused_computation.3 | custom fusion | bytes 7925760 | tf_op jit(solution)/shard_map/gather | solution.py:67
  177.5 0.0 copy-start
  177.5 0.0 copy-start.1
  177.5 3.9 reduce_sum.19
  181.4 0.0 copy-done
  181.4 0.0 copy-done.1
  181.4 0.0 copy-start.2
  181.4 0.0 copy-start.4
  181.5 5.1 %fusion = f32[1024,1024]{1,0:T(8,128)} fusion(f32[64,1024]{1,0:T(8,128)S(1)} %copy-done, f32[64,1024]{1,0:T(8,128)S(1)} %copy-done.1, f32[1024,64]{1,0:T(8,128)S(1)} %broadcast_multiply_fusion, f32[1024,64]{1,0:T(8,128)S(1)} %gather_fusion), kind=kOutput, calls=%fused_computation.7 | convolution fusion | flops 1610874880 | bytes 5242880 | tf_op jit(solution)/shard_map/dot_general | solution.py:27
  186.5 0.0 reduce-scatter.2.cloned.1.call-update
  186.5 0.0 all-gather.2.cloned.1.call-start
  186.6 59.8 %reduce-scatter.2.cloned.1.call-done = f32[64,1024]{1,0:T(8,128)} async-done(((f32[1024,1024]{1,0:T(8,128)}), f32[64,1024]{1,0:T(8,128)}) %reduce-scatter.2.cloned.1.call-update) | async-done | bytes 262160 | tf_op jit(solution)/shard_map/reduce_scatter | solution.py:73
  246.4 0.0 copy-done.2
  246.4 0.0 copy-done.4
  246.4 1.8 multiply_convert_fusion
  248.2 0.0 all-gather.2.cloned.1.call-update
  248.2 0.0 all-reduce.2.cloned.1.call-start
  248.3 41.5 %all-gather.2.cloned.1.call-done = bf16[1024,1024]{1,0:T(8,128)(2,1)} async-done(((bf16[64,1024]{1,0:T(8,128)(2,1)}), bf16[1024,1024]{1,0:T(8,128)(2,1)}) %all-gather.2.cloned.1.call-update) | async-done | bytes 2097168 | tf_op jit(solution)/shard_map/all_gather | solution.py:79
  289.8 3.7 fusion.4
  293.4 0.0 all-reduce.2.cloned.1.call-update
  293.4 94.4 %all-reduce.2.cloned.1.call-done = f32[128,1024]{1,0:T(8,128)} async-done(((f32[128,1024]{1,0:T(8,128)}), f32[128,1024]{1,0:T(8,128)}) %all-reduce.2.cloned.1.call-update) | async-done | bytes 524304 | tf_op jit(solution)/shard_map/psum | solution.py:81
  387.9 1.9 fusion.14
  (7 shorter events, 0.1 us)
Async XLA Ops:
  15.9 14.5 %all-to-all-start = ((s32[16,1,8]{2,1,0:T(1,128)}), s32[16,1,8]{2,1,0:T(1,128)S(1)}, u32[]{:S(2)}, u32[]{:S(2)}) async-start(s32[16,1,8]{2,1,0:T(1,128)} %copy.24), calls=%async_computation | async-start | bytes 16384 | tf_op jit(solution)/shard_map/all_to_all | solution.py:58
  45.0 4.7 %copy-start.5 = (s32[1024]{0:T(1024)S(1)}, s32[1024]{0:T(1024)}, u32[]{:S(2)}) copy-start(s32[1024]{0:T(1024)} %param.11) | copy-start | bytes 12292
  45.0 4.7 %copy-start.3 = (s32[15,1024]{1,0:T(8,128)S(1)}, s32[15,1024]{1,0:T(8,128)}, u32[]{:S(2)}) copy-start(s32[15,1024]{1,0:T(8,128)} %param.12) | copy-start | bytes 184324
  45.1 65.7 %all-to-all-start.1 = ((f32[16,8,128,64]{2,3,1,0:T(8,128)}), f32[16,8,128,64]{2,3,1,0:T(8,128)}, u32[]{:S(2)}, u32[]{:S(2)}) async-start(f32[16,8,128,64]{2,3,1,0:T(8,128)} %bitcast.40), calls=%async_computation.1 | async-start | bytes 8388608 | tf_op jit(solution)/shard_map/all_to_all | solution.py:62
  49.7 196.7 %reduce-scatter.2.cloned.1.call-start = ((), (), s32[]{:S(2)}) async-start(), calls=%async_computation.3 | async-start | bytes 4456448 | tf_op jit(solution)/shard_map/reduce_scatter | solution.py:73
  177.5 4.0 copy-start
  177.5 4.0 %copy-start.1 = (f32[64,1024]{1,0:T(8,128)S(1)}, f32[64,1024]{1,0:T(8,128)}, u32[]{:S(2)}) copy-start(f32[64,1024]{1,0:T(8,128)} %param.16) | copy-start | bytes 786436
  181.4 65.0 %copy-start.2 = (bf16[64,1024]{1,0:T(8,128)(2,1)S(1)}, bf16[64,1024]{1,0:T(8,128)(2,1)}, u32[]{:S(2)}) copy-start(bf16[64,1024]{1,0:T(8,128)(2,1)} %param.19) | copy-start | bytes 393220
  181.4 65.0 %copy-start.4 = (f32[1024]{0:T(1024)S(1)}, f32[1024]{0:T(1024)}, u32[]{:S(2)}) copy-start(f32[1024]{0:T(1024)} %param.18) | copy-start | bytes 12292
  186.5 103.2 %all-gather.2.cloned.1.call-start = ((), (), s32[]{:S(2)}) async-start(), calls=%async_computation.4 | async-start | bytes 2228224 | tf_op jit(solution)/shard_map/all_gather | solution.py:79
  248.2 139.7 %all-reduce.2.cloned.1.call-start = ((), (), s32[]{:S(2)}) async-start(), calls=%async_computation.5 | async-start | bytes 1048576 | tf_op jit(solution)/shard_map/psum | solution.py:81
Sparse Core Ops, SparseCore 0:
  186.6 59.7 reduce-scatter.1
  248.8 40.9 all-gather.1
  293.6 94.2 all-reduce.1
where the time goes:
time: 397 us; the launch traced here: 396 us
  waiting for transfers between devices  255 us (64%)
  local copies, waits for them, and re-layouts  90.3 us (23%)
  other arithmetic  17 us (4%)
  between operations  13.9 us (4%)
  starting transfers between devices  11.8 us (3%)
  matrix products  8.71 us (2%)
    psum x1, waiting for transfers between devices, body(): grad_total = lax.psum(grad_local, 'dom')  94.4 us
    reduce_scatter x1, waiting for transfers between devices, body(): lax.psum_scatter(product(stacked, weight_cat), 'feat', scatter_dimension=...  59.8 us
    all_to_all x1, waiting for transfers between devices, body(): lax.all_to_all(outgoing, 'dom', split_axis=0, concat_axis=0, tiled=True)  55.8 us
    gather x1, local copies, waits for them, and re-layouts, body(): frontier[neighbours.reshape(-1)].reshape(fanout, seeds_dev, cols_dev)  53.7 us
    all_gather x1, waiting for transfers between devices, body(): lax.all_gather(slope, 'feat', axis=0, tiled=True).astype(jnp.float32)  41.5 us
    gather x2, local copies, waits for them, and re-layouts, body(): block_rows[requested.reshape(-1)].reshape(n_dom, SLOTS, BLOCK, cols_dev)  13.3 us
  transfers between devices with their start and end apart: 5, of which 5 were waited for; matrix products, arithmetic and copies ran while one was open for 2% of the time, Pallas kernels for 0%

commit v1 on v0

--- a/solution.py
+++ b/solution.py
@@ -78,7 +78,7 @@
     grad_local = contract(
         stacked, lax.all_gather(slope, "feat", axis=0, tiled=True).astype(jnp.float32)
     )
-    grad_total = lax.psum(grad_local, "dom")
+    grad_total = jnp.sum(lax.all_gather(grad_local, "dom"), axis=0)
     return (hidden, grad_total[:cols_dev], grad_total[cols_dev:])
 
 

time: 397 us -> 382 us (0.962)
  waiting for transfers between devices: 255 us -> 235 us
  other arithmetic: 17 us -> 21.2 us
    psum x1 -> x0, waiting for transfers between devices: 94.4 us -> none  [body(): grad_total = lax.psum(grad_local, 'dom')]
    all_gather x0 -> x1, waiting for transfers between devices: none -> 75 us  [body(): grad_total = jnp.sum(lax.all_gather(grad_local, 'dom'), axis=0)]
    reduce_sum x0 -> x1, other arithmetic: none -> 4.24 us  [body(): grad_total = jnp.sum(lax.all_gather(grad_local, 'dom'), axis=0)]
  transfers between devices with their start and end apart: 5 -> 5, of which waited for: 5 -> 5; matrix products, arithmetic and copies ran while one was open for 2% -> 3% of each run, Pallas kernels for 0% -> 0%
where the time goes in v1:
time: 382 us; the launch traced here: 380 us
  waiting for transfers between devices  235 us (62%)
  local copies, waits for them, and re-layouts  89.2 us (23%)
  other arithmetic  21.2 us (6%)
  between operations  13.9 us (4%)
  starting transfers between devices  11.8 us (3%)
  matrix products  8.77 us (2%)
    all_gather x1, waiting for transfers between devices, body(): grad_total = jnp.sum(lax.all_gather(grad_local, 'dom'), axis=0)  75 us
    reduce_scatter x1, waiting for transfers between devices, body(): lax.psum_scatter(product(stacked, weight_cat), 'feat', scatter_dimension=...  59.8 us
    all_to_all x1, waiting for transfers between devices, body(): lax.all_to_all(outgoing, 'dom', split_axis=0, concat_axis=0, tiled=True)  55.8 us
    gather x1, local copies, waits for them, and re-layouts, body(): frontier[neighbours.reshape(-1)].reshape(fanout, seeds_dev, cols_dev)  53.7 us
    all_gather x1, waiting for transfers between devices, body(): lax.all_gather(slope, 'feat', axis=0, tiled=True).astype(jnp.float32)  41.5 us
    gather x2, local copies, waits for them, and re-layouts, body(): block_rows[requested.reshape(-1)].reshape(n_dom, SLOTS, BLOCK, cols_dev)  13.3 us
  transfers between devices with their start and end apart: 5, of which 5 were waited for; matrix products, arithmetic and copies ran while one was open for 3% of the time, Pallas kernels for 0%

profile of v1, /device:TPU:32, one launch (start us, length us, event | category | flops | bytes accessed | tf_op | source)
XLA Modules:
  0.0 380.1 jit_solution(10203172342695699570)
XLA Ops:
  7.2 0.7 fusion.5
  7.9 0.1 reduce_window_sum.11
  8.0 0.8 select_reduce_fusion
  8.8 0.7 fusion.10
  9.5 5.7 %scatter_fusion = s32[16,8]{0,1:T(8,128)S(1)} fusion(s32[16,8]{0,1:T(8,128)S(1)} %broadcast_in_dim.18, s32[64]{0:T(128)S(1)} %get-tuple-element.8, s32[64]{0:T(128)} %param.14), kind=kCustom, calls=%fused_computation.4 | custom fusion | bytes 1280 | tf_op jit(solution)/shard_map/scatter | solution.py:57
  15.3 0.7 copy.24
  15.9 7.0 %all-to-all-start = ((s32[16,1,8]{2,1,0:T(1,128)}), s32[16,1,8]{2,1,0:T(1,128)S(1)}, u32[]{:S(2)}, u32[]{:S(2)}) async-start(s32[16,1,8]{2,1,0:T(1,128)} %copy.24), calls=%async_computation | async-start | bytes 16384 | tf_op jit(solution)/shard_map/all_to_all | solution.py:58
  23.0 0.7 fusion.6
  23.7 3.8 copy.23
  27.5 2.9 all-to-all-done
  30.4 0.5 broadcast.144
  31.0 0.7 reduce.3
  31.6 0.1 reshape.132
  31.7 6.5 %gather_fusion.1 = f32[128,128,64]{2,1,0:T(8,128)} fusion(f32[64,128,64]{2,1,0:T(8,128)} %bitcast.38, s32[1024]{0:T(1024)S(1)} %pad_clamp_fusion.1), kind=kCustom, calls=%fused_computation.1 | custom fusion | bytes 8389120 | tf_op jit(solution)/shard_map/gather | solution.py:61
  38.2 6.8 %copy.25 = f32[128,128,64]{1,2,0:T(8,128)} copy(f32[128,128,64]{2,1,0:T(8,128)} %gather_fusion.1) | data formatting | bytes 8388608 | tf_op jit(solution)/shard_map/gather | solution.py:61
  45.0 0.0 copy-start.5
  45.0 0.0 copy-start.3
  45.1 4.7 %all-to-all-start.1 = ((f32[16,8,128,64]{2,3,1,0:T(8,128)}), f32[16,8,128,64]{2,3,1,0:T(8,128)}, u32[]{:S(2)}, u32[]{:S(2)}) async-start(f32[16,8,128,64]{2,3,1,0:T(8,128)} %bitcast.41), calls=%async_computation.1 | async-start | bytes 8388608 | tf_op jit(solution)/shard_map/all_to_all | solution.py:62
  49.7 0.0 reduce-scatter.2.cloned.1.call-start
  49.8 0.0 copy-done.5
  49.8 0.0 copy-done.3
  49.8 0.1 copy.30
  49.9 5.0 %gather_fusion = f32[1024,64]{1,0:T(8,128)S(1)} fusion(f32[8192,64]{1,0:T(8,128)} %bitcast.39, s32[1024]{0:T(1024)S(1)} %fusion.7), kind=kCustom, calls=%fused_computation | custom fusion | bytes 528384 | tf_op jit(solution)/shard_map/gather | solution.py:69
  54.9 0.1 compare_select_fusion
  55.0 55.8 %all-to-all-done.1 = f32[16,8,128,64]{2,3,1,0:T(8,128)} async-done(((f32[16,8,128,64]{2,3,1,0:T(8,128)}), f32[16,8,128,64]{2,3,1,0:T(8,128)}, u32[]{:S(2)}, u32[]{:S(2)}) %all-to-all-start.1) | async-done | bytes 4194336 | tf_op jit(solution)/shard_map/all_to_all | solution.py:62
  110.8 2.9 gather_fusion.2
  113.7 2.7 copy.28
  116.4 7.4 %bitcast_select_fusion = f32[8192,64]{1,0:T(8,128)} fusion(f32[64,128,64]{2,1,0:T(8,128)} %copy.28, pred[8192]{0:T(1024)(128)(4,1)S(1)} %fusion.6), kind=kLoop, calls=%fused_computation.5 | loop fusion | flops 524288 | bytes 4202496 | tf_op jit(solution)/shard_map/jit(_where)/select_n | solution.py:66
  123.8 53.7 %gather_fusion.3 = f32[15360,64]{1,0:T(8,128)} fusion(f32[8192,64]{1,0:T(8,128)} %bitcast_select_fusion, s32[15360]{0:T(1024)S(1)} %broadcast_clamp_fusion), kind=kCustom, calls=%fused_computation.3 | custom fusion | bytes 7925760 | tf_op jit(solution)/shard_map/gather | solution.py:67
  177.5 0.0 copy-start
  177.5 0.0 copy-start.1
  177.5 3.9 %reduce_sum.28 = f32[1024,64]{1,0:T(8,128)S(1)} reduce(f32[15,1024,64]{2,1,0:T(8,128)} %bitcast.40, f32[]{:T(128)} %constant.7.clone.1), dimensions={0}, to_apply=%region_3.4 | reduce | flops 917504 | bytes 4194308 | tf_op jit(solution)/shard_map/reduce_sum | solution.py:68
  181.4 0.0 copy-done
  181.4 0.0 copy-done.1
  181.4 0.0 copy-start.2
  181.4 0.0 copy-start.4
  181.5 5.1 %fusion = f32[1024,1024]{1,0:T(8,128)} fusion(f32[64,1024]{1,0:T(8,128)S(1)} %copy-done, f32[64,1024]{1,0:T(8,128)S(1)} %copy-done.1, f32[1024,64]{1,0:T(8,128)S(1)} %broadcast_multiply_fusion, f32[1024,64]{1,0:T(8,128)S(1)} %gather_fusion), kind=kOutput, calls=%fused_computation.7 | convolution fusion | flops 1610874880 | bytes 5242880 | tf_op jit(solution)/shard_map/dot_general | solution.py:27
  186.5 0.0 reduce-scatter.2.cloned.1.call-update
  186.5 0.0 all-gather.4.cloned.1.call-start
  186.6 59.8 %reduce-scatter.2.cloned.1.call-done = f32[64,1024]{1,0:T(8,128)} async-done(((f32[1024,1024]{1,0:T(8,128)}), f32[64,1024]{1,0:T(8,128)}) %reduce-scatter.2.cloned.1.call-update) | async-done | bytes 262160 | tf_op jit(solution)/shard_map/reduce_scatter | solution.py:73
  246.4 0.0 copy-done.2
  246.4 0.0 copy-done.4
  246.4 1.8 multiply_convert_fusion
  248.2 0.0 all-gather.4.cloned.1.call-update
  248.2 0.0 all-gather.6.cloned.1.call-start
  248.3 41.5 %all-gather.4.cloned.1.call-done = bf16[1024,1024]{1,0:T(8,128)(2,1)} async-done(((bf16[64,1024]{1,0:T(8,128)(2,1)}), bf16[1024,1024]{1,0:T(8,128)(2,1)}) %all-gather.4.cloned.1.call-update) | async-done | bytes 2097168 | tf_op jit(solution)/shard_map/all_gather | solution.py:79
  289.8 3.7 fusion.4
  293.5 0.0 all-gather.6.cloned.1.call-update
  293.5 75.0 %all-gather.6.cloned.1.call-done = f32[2048,1024]{1,0:T(8,128)} async-done(((f32[128,1024]{1,0:T(8,128)}), f32[2048,1024]{1,0:T(8,128)}) %all-gather.6.cloned.1.call-update) | async-done | bytes 8388624 | tf_op jit(solution)/shard_map/all_gather | solution.py:81
  368.5 4.2 %reduce_sum.29 = f32[128,1024]{1,0:T(8,128)S(1)} reduce(f32[16,128,1024]{2,1,0:T(8,128)} %bitcast.42, f32[]{:T(128)} %constant.7.clone.1), dimensions={0}, to_apply=%region_5.6 | reduce | flops 1966080 | bytes 8912900 | tf_op jit(solution)/shard_map/reduce_sum | solution.py:81
  372.7 0.8 fusion.14
  (7 shorter events, 0.1 us)
Async XLA Ops:
  15.9 14.5 %all-to-all-start = ((s32[16,1,8]{2,1,0:T(1,128)}), s32[16,1,8]{2,1,0:T(1,128)S(1)}, u32[]{:S(2)}, u32[]{:S(2)}) async-start(s32[16,1,8]{2,1,0:T(1,128)} %copy.24), calls=%async_computation | async-start | bytes 16384 | tf_op jit(solution)/shard_map/all_to_all | solution.py:58
  45.0 4.7 %copy-start.5 = (s32[1024]{0:T(1024)S(1)}, s32[1024]{0:T(1024)}, u32[]{:S(2)}) copy-start(s32[1024]{0:T(1024)} %param.11) | copy-start | bytes 12292
  45.0 4.7 %copy-start.3 = (s32[15,1024]{1,0:T(8,128)S(1)}, s32[15,1024]{1,0:T(8,128)}, u32[]{:S(2)}) copy-start(s32[15,1024]{1,0:T(8,128)} %param.12) | copy-start | bytes 184324
  45.1 65.7 %all-to-all-start.1 = ((f32[16,8,128,64]{2,3,1,0:T(8,128)}), f32[16,8,128,64]{2,3,1,0:T(8,128)}, u32[]{:S(2)}, u32[]{:S(2)}) async-start(f32[16,8,128,64]{2,3,1,0:T(8,128)} %bitcast.41), calls=%async_computation.1 | async-start | bytes 8388608 | tf_op jit(solution)/shard_map/all_to_all | solution.py:62
  49.7 196.7 %reduce-scatter.2.cloned.1.call-start = ((), (), s32[]{:S(2)}) async-start(), calls=%async_computation.3 | async-start | bytes 4456448 | tf_op jit(solution)/shard_map/reduce_scatter | solution.py:73
  177.5 4.0 %copy-start = (f32[64,1024]{1,0:T(8,128)S(1)}, f32[64,1024]{1,0:T(8,128)}, u32[]{:S(2)}) copy-start(f32[64,1024]{1,0:T(8,128)} %param.17) | copy-start | bytes 786436
  177.5 4.0 %copy-start.1 = (f32[64,1024]{1,0:T(8,128)S(1)}, f32[64,1024]{1,0:T(8,128)}, u32[]{:S(2)}) copy-start(f32[64,1024]{1,0:T(8,128)} %param.16) | copy-start | bytes 786436
  181.4 65.0 %copy-start.2 = (bf16[64,1024]{1,0:T(8,128)(2,1)S(1)}, bf16[64,1024]{1,0:T(8,128)(2,1)}, u32[]{:S(2)}) copy-start(bf16[64,1024]{1,0:T(8,128)(2,1)} %param.19) | copy-start | bytes 393220
  181.4 65.0 %copy-start.4 = (f32[1024]{0:T(1024)S(1)}, f32[1024]{0:T(1024)}, u32[]{:S(2)}) copy-start(f32[1024]{0:T(1024)} %param.18) | copy-start | bytes 12292
  186.5 103.2 %all-gather.4.cloned.1.call-start = ((), (), s32[]{:S(2)}) async-start(), calls=%async_computation.4 | async-start | bytes 2228224 | tf_op jit(solution)/shard_map/all_gather | solution.py:79
  248.2 120.3 %all-gather.6.cloned.1.call-start = ((), (), s32[]{:S(2)}) async-start(), calls=%async_computation.5 | async-start | bytes 8912896 | tf_op jit(solution)/shard_map/all_gather | solution.py:81
Sparse Core Ops, SparseCore 0:
  186.6 59.7 reduce-scatter.1
  248.8 40.9 all-gather.3
  293.6 74.7 all-gather.5
